TPU v7x, 32 devices: a whole 2x2x4 slice. The times are simulated.
32 devices in a mesh: row: 8 (over z, y), col: 4 (over x, core).
Axes of the slice: x: 2, y: 2, z: 4, core: 2. Of those that a mesh axis runs over, the one named last changes fastest.
Arguments:
- coeffs: float32 [16384, 2048], P('row', 'col'), may hold values from -0.4375 to 0.4375
- pattern: int32 [256, 32], P('row', 'col'), may hold values from 0 to 1, as said below
Outputs:
- band: float32 [32, 3, 512, 512], P(('row', 'col'))
Inputs may be any that keep to these rules, and one draw needn't show every extreme that they name: Orbital locality: with c = (a * 32) // 256, pattern[a, b] is 0 unless the circular distance min((b - c) mod 32, (c - b) mod 32) is at most 4. Some block row keeps a block at distance exactly 4 (where 32 allows it); no other structure is promised.
All inputs are finite; a program needn't handle non-finite values.
Results may differ from a plain program's by a relative error of at most 0.0003.
Values sent between devices are 32-bit elements; how exact they have to be, the bound alone decides.
A program may use at most 128 MiB of HBM per device.

v0:
```python
import jax
import jax.numpy as jnp
from jax import lax
from jax.sharding import PartitionSpec as P

BLOCK = 64
STEPS = 3


def passed_along(x, axis, by):
    size = lax.axis_size(axis)
    return lax.ppermute(x, axis, [(i, (i + by) % size) for i in range(size)])


def band_rows(own, near, steps):
    width = own.shape[0]
    product = jnp.dot(
        own, near.T, precision=lax.Precision.HIGHEST, preferred_element_type=jnp.float32
    )
    return product.reshape(width, steps, width).transpose(1, 0, 2)


def shards(coeffs, pattern):
    rows, cols = coeffs.shape
    shaped = coeffs.reshape(rows // BLOCK, BLOCK, cols // BLOCK, BLOCK)
    masked = (shaped * pattern.astype(jnp.float32)[:, None, :, None]).reshape(rows, cols)
    mine = lax.all_to_all(masked, "col", split_axis=0, concat_axis=1, tiled=True)
    pieces = [mine]
    current = mine
    for offset in range(1, STEPS):
        current = passed_along(current, ("row", "col"), -1)
        pieces.append(current)
    near = jnp.concatenate(pieces, axis=0)
    return band_rows(mine, near, STEPS)[None]


def solution(mesh):
    in_specs = (P("row", "col"), P("row", "col"))
    out_specs = P(("row", "col"), None, None, None)
    return jax.shard_map(shards, mesh=mesh, in_specs=in_specs, out_specs=out_specs, check_vma=False)
```

profile of v0, /device:TPU:0, one launch (start us, length us, event | category | flops | bytes accessed | tf_op | source)
XLA Modules:
  0.0 200.7 jit_solution(290701903610158782)
XLA Ops:
  0.0 0.7 convert_element_type.3
  0.7 0.1 copy.5
  0.8 3.8 %mul.11 = f32[32,64,8,64]{3,2,1,0:T(8,128)} broadcast(f32[32,8]{1,0:T(8,128)S(1)} %copy.5), dimensions={0,2} | broadcast | bytes 4195328 | tf_op jit(solution)/shard_map/mul | solution.py:26
  4.6 7.5 %mul.12 = f32[2048,512]{1,0:T(8,128)} reshape(f32[32,64,8,64]{3,2,1,0:T(8,128)} %mul.11) | data formatting | bytes 8388608 | tf_op jit(solution)/shard_map/mul | solution.py:26
  12.1 4.5 %mul.13 = f32[2048,512]{1,0:T(8,128)S(1)} multiply(f32[2048,512]{1,0:T(8,128)} %param.2, f32[2048,512]{1,0:T(8,128)} %mul.12) | non-fusion elementwise | flops 1048576 | bytes 12582912 | tf_op jit(solution)/shard_map/mul | solution.py:26
  16.6 52.2 %all_to_all.19 = f32[4,512,512]{2,1,0:T(8,128)S(1)} all-to-all(f32[4,512,512]{2,1,0:T(8,128)S(1)} %bitcast.15), channel_id=1, replica_groups=mesh['row'=8,'col'=4] {'col'}, dimensions={0} | all-to-all | bytes 8388608 | tf_op jit(solution)/shard_map/all_to_all | solution.py:27
  68.7 0.4 copy.7
  69.2 0.0 copy-start
  69.2 1.9 copy-done
  71.1 3.9 %collective-permute-start = (f32[512,2048]{1,0:T(8,128)S(1)}, f32[512,2048]{1,0:T(8,128)}, u32[]{:S(2)}, u32[]{:S(2)}) collective-permute-start(f32[512,2048]{1,0:T(8,128)S(1)} %bitcast.16), channel_id=1, source_target_pairs={{0,31},{1,0},{2,1},{3,2},{4,3},{5,4},{6,5},{7,6},{8,7},{9,8},{10,9... | collective-permute-start | bytes 12582920 | tf_op jit(solution)/shard_map/ppermute | solution.py:12
  75.0 46.0 %collective-permute-done = f32[512,2048]{1,0:T(8,128)} collective-permute-done((f32[512,2048]{1,0:T(8,128)S(1)}, f32[512,2048]{1,0:T(8,128)}, u32[]{:S(2)}, u32[]{:S(2)}) %collective-permute-start) | collective-permute-done | bytes 4194336 | tf_op jit(solution)/shard_map/ppermute | solution.py:12
  121.0 5.6 %collective-permute-start.1 = (f32[512,2048]{1,0:T(8,128)}, f32[512,2048]{1,0:T(8,128)}, u32[]{:S(2)}, u32[]{:S(2)}) collective-permute-start(f32[512,2048]{1,0:T(8,128)} %collective-permute-done), channel_id=1, source_target_pairs={{0,31},{1,0},{2,1},{3,2},{4,3},{5,4},{6,5},{7,6},{8,7},{9,8},{10,9... | collective-permute-start | bytes 12582920 | tf_op jit(solution)/shard_map/ppermute | solution.py:12
  126.6 4.6 %copy.6 = f32[512,4,512]{2,1,0:T(4,128)} copy(f32[512,4,512]{2,0,1:T(8,128)S(1)} %bitcast.14) | data formatting | bytes 8388608 | tf_op jit(solution)/shard_map/all_to_all | solution.py:27
  131.3 6.0 %reshape.9 = f32[512,2048,1]{1,0,2:T(8,128)} reshape(f32[512,4,512]{2,1,0:T(4,128)} %copy.6) | data formatting | bytes 8388608 | tf_op jit(solution)/shard_map/all_to_all | solution.py:27
  137.3 0.0 copy-start.1
  137.3 35.7 %collective-permute-done.1 = f32[512,2048]{1,0:T(8,128)} collective-permute-done((f32[512,2048]{1,0:T(8,128)}, f32[512,2048]{1,0:T(8,128)}, u32[]{:S(2)}, u32[]{:S(2)}) %collective-permute-start.1) | collective-permute-done | bytes 4194336 | tf_op jit(solution)/shard_map/ppermute | solution.py:12
  173.0 5.5 %pad_maximum_fusion = f32[1536,2048]{1,0:T(8,128)S(1)} fusion(f32[512,2048]{1,0:T(8,128)} %collective-permute-done.1, f32[512,2048]{1,0:T(8,128)} %collective-permute-done, f32[512,2048]{1,0:T(8,128)} %bitcast.17), kind=kLoop, calls=%fused_computation | loop fusion | flops 6291456 | bytes 25165824 | tf_op jit(solution)/shard_map/concatenate | solution.py:33
  178.5 0.0 copy-done.1
  178.5 22.2 %convolution_bitcast_fusion = f32[1,3,512,512]{3,2,1,0:T(8,128)} fusion(f32[512,2048,1]{1,0,2:T(8,128)S(1)} %copy-done.1, f32[3,512,2048]{2,1,0:T(8,128)S(1)} %bitcast.18), kind=kOutput, calls=%fused_computation.1 | convolution fusion | flops 19327352832 | bytes 19922944 | tf_op jit(solution)/shard_map/dot_general | solution.py:17
Async XLA Ops:
  69.2 1.9 copy-start
  71.1 49.9 %collective-permute-start = (f32[512,2048]{1,0:T(8,128)S(1)}, f32[512,2048]{1,0:T(8,128)}, u32[]{:S(2)}, u32[]{:S(2)}) collective-permute-start(f32[512,2048]{1,0:T(8,128)S(1)} %bitcast.16), channel_id=1, source_target_pairs={{0,31},{1,0},{2,1},{3,2},{4,3},{5,4},{6,5},{7,6},{8,7},{9,8},{10,9... | collective-permute-start | bytes 12582920 | tf_op jit(solution)/shard_map/ppermute | solution.py:12
  121.0 51.9 %collective-permute-start.1 = (f32[512,2048]{1,0:T(8,128)}, f32[512,2048]{1,0:T(8,128)}, u32[]{:S(2)}, u32[]{:S(2)}) collective-permute-start(f32[512,2048]{1,0:T(8,128)} %collective-permute-done), channel_id=1, source_target_pairs={{0,31},{1,0},{2,1},{3,2},{4,3},{5,4},{6,5},{7,6},{8,7},{9,8},{10,9... | collective-permute-start | bytes 12582920 | tf_op jit(solution)/shard_map/ppermute | solution.py:12
  137.3 41.2 %copy-start.1 = (f32[512,2048,1]{1,0,2:T(8,128)S(1)}, f32[512,2048,1]{1,0,2:T(8,128)}, u32[]{:S(2)}) copy-start(f32[512,2048,1]{1,0,2:T(8,128)} %reshape.9) | copy-start | bytes 12582916
where the time goes:
time: 201 us
  waiting for transfers between devices  81.7 us (41%)
  blocking collectives  52.2 us (26%)
  local copies, waits for them, and re-layouts  24.4 us (12%)
  matrix products  22.2 us (11%)
  other arithmetic  10.7 us (5%)
  starting transfers between devices  9.47 us (5%)
    ppermute x2, waiting for transfers between devices, passed_along(): return lax.ppermute(x, axis, [(i, (i + by) % size) for i in range(size)])  81.7 us
    all_to_all x1, blocking collectives, shards(): lax.all_to_all(masked, 'col', split_axis=0, concat_axis=1, tiled=True)  52.2 us
    dot_general x1, matrix products, band_rows(): jnp.dot(own, near.T, precision=lax.Precision.HIGHEST, preferred_element_t...  22.2 us
    mul x2, local copies, waits for them, and re-layouts, shards(): shaped * pattern.astype(jnp.float32)[:, None, :, None]  11.3 us
    all_to_all x3, local copies, waits for them, and re-layouts, shards(): lax.all_to_all(masked, 'col', split_axis=0, concat_axis=1, tiled=True)  11.1 us
    ppermute x2, starting transfers between devices, passed_along(): return lax.ppermute(x, axis, [(i, (i + by) % size) for i in range(size)])  9.47 us
    concatenate x1, other arithmetic, shards(): near = jnp.concatenate(pieces, axis=0)  5.53 us
    mul x1, other arithmetic, shards(): shaped * pattern.astype(jnp.float32)[:, None, :, None]  4.48 us
  transfers between devices with their start and end apart: 2, of which 2 were waited for; matrix products, arithmetic and copies ran while one was open for 5% of the time, Pallas kernels for 0%

commit v1 on v0

v1 whole, which is shorter than its diff:
```python
import functools

import jax
import jax.numpy as jnp
from jax import lax
from jax.experimental import pallas as pl
from jax.experimental.pallas import tpu as pltpu
from jax.sharding import PartitionSpec as P

BLOCK = 64
STEPS = 3
REACH = 4
LANES = 128
MESH = pl.DeviceIdType.MESH


def kernel(
    nrow, ncol, nbr, nbo, coeffs_ref, pattern_ref, out_ref, stage, recv, left, right,
    load_sem, send_sem, recv_sem, pass_sem,
):
    r, k = lax.axis_index("row"), lax.axis_index("col")
    core = k % 2
    nsub = nrow * ncol
    width = stage.shape[2]
    per = coeffs_ref.shape[1] // LANES
    ntile = nbo * BLOCK // LANES
    span = recv.shape[1]
    blocks = width // BLOCK
    late = 1 if blocks * nbo == nbr else 0

    def first_tile(g):
        center = g * blocks * nbo // nbr
        return (center + nbo - REACH) // 2 % ntile

    loads = lambda l, t: pltpu.make_async_copy(
        coeffs_ref.at[pl.ds(l * width, width), pl.ds(t * LANES, LANES)], stage.at[l, t], load_sem.at[l, t]
    )
    for l in range(ncol):
        for t in range(per):
            loads(l, t).start()

    up, down = (r + 1) % nrow, (r + nrow - 1) % nrow
    barrier = pltpu.get_barrier_semaphore()
    for d in range(1, ncol):
        pl.semaphore_signal(barrier, inc=1, device_id=(r, (k + d) % ncol), device_id_type=MESH)
    for d in range(ncol):
        pl.semaphore_signal(barrier, inc=1, device_id=(up, (k + d) % ncol), device_id_type=MESH)
        pl.semaphore_signal(barrier, inc=1, device_id=(down, (k + d) % ncol), device_id_type=MESH)

    lane = lax.broadcasted_iota(jnp.int32, (1, LANES), 1)

    def mask(l, t):
        for b in range(blocks):
            p0 = pattern_ref[l * blocks + b, 2 * t].astype(jnp.float32)
            p1 = pattern_ref[l * blocks + b, 2 * t + 1].astype(jnp.float32)
            rows = pl.ds(b * BLOCK, BLOCK)
            stage[l, t, rows, :] = stage[l, t, rows, :] * jnp.where(lane < BLOCK, p0, p1)

    def target(l, t, c):
        h = l % 2 + 2 * c
        base = (r * ncol + l - h + nsub) % nsub
        j = (k * per + t - first_tile(base) + ntile) % ntile
        wanted = jnp.logical_and(j < span, j >= late * c)
        row, col = base // ncol, base % ncol + l % 2
        here = jnp.logical_and(row == r, col == k)
        j = jnp.minimum(j, span - 1)
        return h, j, row, col, jnp.logical_and(wanted, here), jnp.logical_and(wanted, jnp.logical_not(here))

    def send(l, t, c):
        h, j, row, col, local, remote = target(l, t, c)
        move = pltpu.make_async_remote_copy(
            stage.at[l, t], recv.at[h, j], send_sem.at[l, t, c], recv_sem.at[h, j],
            device_id=(row, col), device_id_type=MESH,
        )
        return local, remote, pltpu.make_async_copy(stage.at[l, t], recv.at[h, j], recv_sem.at[h, j]), move

    def mask_all(l, carry):
        for t in range(per):
            loads(l, t).wait()
            mask(l, t)
        return carry

    lax.fori_loop(0, ncol, mask_all, 0)
    pl.semaphore_wait(barrier, 3 * ncol - 1)

    def send_all(l, carry):
        for t in range(per):
            for c in range(2):
                local, remote, own, move = send(l, t, c)
                pl.when(local)(own.start)
                pl.when(remote)(move.start)
        return carry

    lax.fori_loop(0, ncol, send_all, 0)
    out_ref[...] = jnp.zeros_like(out_ref)

    def pass_on(h, j):
        return pltpu.make_async_remote_copy(
            recv.at[h, j], recv.at[h, j], pass_sem.at[j], recv_sem.at[h, j],
            device_id=(r, k + 1 - 2 * core), device_id_type=MESH,
        )

    shared, alone = 2 - core, 3 * core

    def arrived(h, j):
        pl.when(j >= jnp.where(h < 2, 0, late))(pass_on(h, j).wait_recv)

    def multiply(j, carry):
        has_shared = j >= jnp.where(shared < 2, 0, late)
        arrived(shared, j)
        pl.when(has_shared)(pass_on(shared, j).start)
        arrived(alone, j)
        arrived(1 + core, j)
        for step in range(STEPS):
            h = core + step

            @pl.when(j >= jnp.where(h < 2, 0, late))
            def _():
                x = recv[h, j]
                high = x.astype(jnp.bfloat16)
                low = (x - high.astype(jnp.float32)).astype(jnp.bfloat16)
                if step == 0:
                    left[:, 0:LANES] = high
                    left[:, LANES:2 * LANES] = low
                    left[:, 2 * LANES:3 * LANES] = high
                right[:, 0:LANES] = high
                right[:, LANES:2 * LANES] = high
                right[:, 2 * LANES:3 * LANES] = low

                def part(i, carry):
                    rows = pl.ds(pl.multiple_of(i * LANES, LANES), LANES)
                    out_ref[0, step, rows, :] += lax.dot_general(
                        left[rows, :], right[...], (((1,), (1,)), ((), ())),
                        preferred_element_type=jnp.float32,
                    )
                    return carry

                lax.fori_loop(0, width // LANES, part, 0)

        return carry

    lax.fori_loop(0, span, multiply, 0)

    def sent_all(l, carry):
        for t in range(per):
            for c in range(2):
                _, remote, _, move = send(l, t, c)
                pl.when(remote)(move.wait_send)
        return carry

    lax.fori_loop(0, ncol, sent_all, 0)

    def passed_all(j, carry):
        pl.when(j >= jnp.where(shared < 2, 0, late))(pass_on(shared, j).wait_send)
        return carry

    lax.fori_loop(0, span, passed_all, 0)


def shards(nrow, ncol, coeffs, pattern):
    rows, cols = coeffs.shape
    width = rows // ncol
    nbr, nbo = pattern.shape[0] * nrow, pattern.shape[1] * ncol
    per = cols // LANES
    span = REACH + 1
    return pl.pallas_call(
        functools.partial(kernel, nrow, ncol, nbr, nbo),
        out_shape=jax.ShapeDtypeStruct((1, STEPS, width, width), jnp.float32),
        in_specs=[pl.BlockSpec(memory_space=pl.ANY), pl.BlockSpec(memory_space=pltpu.SMEM)],
        out_specs=pl.BlockSpec(memory_space=pltpu.VMEM),
        scratch_shapes=[
            pltpu.VMEM((ncol, per, width, LANES), jnp.float32),
            pltpu.VMEM((4, span, width, LANES), jnp.float32),
            pltpu.VMEM((width, 3 * LANES), jnp.bfloat16),
            pltpu.VMEM((width, 3 * LANES), jnp.bfloat16),
            pltpu.SemaphoreType.DMA((ncol, per)),
            pltpu.SemaphoreType.DMA((ncol, per, 2)),
            pltpu.SemaphoreType.DMA((4, span)),
            pltpu.SemaphoreType.DMA((span,)),
        ],
        compiler_params=pltpu.CompilerParams(
            collective_id=0, has_side_effects=True, vmem_limit_bytes=40 << 20
        ),
        cost_estimate=pl.CostEstimate(
            flops=2 * 3 * STEPS * width * width * span * LANES,
            bytes_accessed=4 * (rows * cols + STEPS * width * width), transcendentals=0,
        ),
    )(coeffs, pattern)


def solution(mesh):
    in_specs = (P("row", "col"), P("row", "col"))
    out_specs = P(("row", "col"), None, None, None)
    body = functools.partial(shards, mesh.shape["row"], mesh.shape["col"])
    return jax.shard_map(body, mesh=mesh, in_specs=in_specs, out_specs=out_specs, check_vma=False)
```

time: 201 us -> 78.4 us (0.39)
  the two profiles are of different devices: /device:TPU:0 before, /device:TPU:6 now
where the time goes in v1:
time: 78.4 us; the launch traced here: 78.2 us
  Pallas kernels  73.6 us (94%)
  local copies, waits for them, and re-layouts  4.62 us (6%)
    pallas_call x1, Pallas kernels, shards(): pl.pallas_call(functools.partial(kernel, nrow, ncol, nbr, nbo), out_shape...  73.6 us
    unnamed x4, local copies, waits for them, and re-layouts  4.62 us

profile of v1, /device:TPU:6, one launch (start us, length us, event | category | flops | bytes accessed | tf_op | source)
XLA Modules:
  0.0 78.2 jit_solution(9884203039125500207)
XLA Ops:
  0.0 0.8 copy.3.pattern_ref
  0.8 0.0 copy-start
  0.8 2.2 %copy-done = f32[2048,512]{1,0:T(8,128)S(1)} copy-done((f32[2048,512]{1,0:T(8,128)S(1)}, f32[2048,512]{1,0:T(8,128)}, u32[]{:S(2)}) %copy-start) | copy-done | bytes 4194328
  3.0 73.6 %shard_map.28 = f32[1,3,512,512]{3,2,1,0:T(8,128)S(1)} custom-call(f32[2048,512]{1,0:T(8,128)S(1)} %copy-done, s32[32,8]{1,0:T(8,128)S(1)} %copy.3.pattern_ref), custom_call_target="tpu_custom_call" | custom-call | flops 3019898880 | bytes 7340032 | tf_op jit(solution)/shard_map/pallas_call | solution.py:166
  76.5 1.7 %copy.5 = f32[1,3,512,512]{3,2,1,0:T(8,128)} copy(f32[1,3,512,512]{3,2,1,0:T(8,128)S(1)} %shard_map.28) | data formatting | bytes 6291456
Async XLA Ops:
  0.8 2.2 %copy-start = (f32[2048,512]{1,0:T(8,128)S(1)}, f32[2048,512]{1,0:T(8,128)}, u32[]{:S(2)}) copy-start(f32[2048,512]{1,0:T(8,128)} %coeffs_ref.1) | copy-start | bytes 12582916

commit v2 on v1

--- a/solution.py
+++ b/solution.py
@@ -1,3 +1,4 @@
+import collections
 import functools
 
 import jax
@@ -14,9 +15,86 @@
 MESH = pl.DeviceIdType.MESH
 
 
+def legs(a, b):
+    out, at = [], list(a)
+    for axis in (2, 0, 1):
+        while at[axis] != b[axis]:
+            step = 1 if b[axis] > at[axis] else -1
+            out.append((tuple(at), axis, step))
+            at[axis] += step
+    return out
+
+
+def planned(nrow, ncol, per, width, nbr, nbo, span, late):
+    nsub, ntile, blocks = nrow * ncol, nbo * BLOCK // LANES, width // BLOCK
+    place = lambda row, col: (col // 2, row % 2, row // 2)
+    chips = [(x, y, z) for z in range(nrow // 2) for y in range(2) for x in range(ncol // 2)]
+    tiles = []
+    for g in range(nsub):
+        for k in range(ncol):
+            for t in range(per):
+                for c in range(2):
+                    l = g % ncol
+                    h = l % 2 + 2 * c
+                    base = (g - h) % nsub
+                    first = (base * blocks * nbo // nbr + nbo - REACH) // 2 % ntile
+                    j = (k * per + t - first) % ntile
+                    if late * c <= j < span:
+                        tiles.append((g // ncol, k, l, t, h, j, base // ncol, base % ncol + l % 2))
+    load, choices, chosen = collections.Counter(), [], []
+    for row, k, l, t, h, j, to_row, to_col in tiles:
+        a, b = place(row, k), place(to_row, to_col)
+        ways = [(None, legs(a, b))]
+        for q in chips:
+            if a != b and q != a and q != b and len(legs(a, q)) + len(legs(q, b)) <= 6:
+                ways.append((q, legs(a, q) + legs(q, b)))
+        choices.append(ways)
+        chosen.append(0)
+        load.update(ways[0][1])
+    for _ in range(12):
+        for i, ways in enumerate(choices):
+            load.subtract(ways[chosen[i]][1])
+            costs = [
+                (sum((load[e] + 1) ** 6 - load[e] ** 6 for e in way) + (0 if q is None else 72900), n != chosen[i], n)
+                for n, (q, way) in enumerate(ways)
+            ]
+            chosen[i] = min(costs)[2]
+            load.update(ways[chosen[i]][1])
+    sends = collections.defaultdict(list)
+    relays = collections.defaultdict(list)
+    used = collections.Counter()
+    order = sorted(range(len(tiles)), key=lambda i: (chosen[i] == 0, tiles[i][5], i))
+    for i in order:
+        row, k, l, t, h, j, to_row, to_col = tiles[i]
+        q = choices[i][chosen[i]][0]
+        if q is None:
+            sends[row, k].append((l, t, h, j, to_row, to_col, None))
+        else:
+            via_row, via_col = q[2] * 2 + q[1], q[0] * 2 + used[q] % 2
+            used[q] += 1
+            slot = len(relays[via_row, via_col])
+            sends[row, k].append((l, t, h, j, via_row, via_col, slot))
+            relays[via_row, via_col].append((h, j, to_row, to_col))
+    peers = collections.defaultdict(set)
+    for row in range(nrow):
+        for k in range(0, ncol, 2):
+            peers[row, k].add((row, k + 1))
+            peers[row, k + 1].add((row, k))
+    for a in list(sends):
+        for move in sends[a]:
+            if move[4:6] != a:
+                peers[a].add(move[4:6])
+                peers[move[4:6]].add(a)
+    for a in list(relays):
+        for move in relays[a]:
+            peers[a].add(move[2:4])
+            peers[move[2:4]].add(a)
+    return sends, relays, peers
+
+
 def kernel(
-    nrow, ncol, nbr, nbo, coeffs_ref, pattern_ref, out_ref, stage, recv, left, right,
-    load_sem, send_sem, recv_sem, pass_sem,
+    nrow, ncol, nbr, nbo, plan, coeffs_ref, pattern_ref, out_ref, stage, recv, hold, left, right,
+    load_sem, send_sem, recv_sem, pass_sem, via_sem, hold_sem,
 ):
     r, k = lax.axis_index("row"), lax.axis_index("col")
     core = k % 2
@@ -39,20 +117,30 @@
         for t in range(per):
             loads(l, t).start()
 
-    up, down = (r + 1) % nrow, (r + nrow - 1) % nrow
     barrier = pltpu.get_barrier_semaphore()
-    for d in range(1, ncol):
-        pl.semaphore_signal(barrier, inc=1, device_id=(r, (k + d) % ncol), device_id_type=MESH)
-    for d in range(ncol):
-        pl.semaphore_signal(barrier, inc=1, device_id=(up, (k + d) % ncol), device_id_type=MESH)
-        pl.semaphore_signal(barrier, inc=1, device_id=(down, (k + d) % ncol), device_id_type=MESH)
+    me = r * ncol + k
+    if plan is None:
+        up, down = (r + 1) % nrow, (r + nrow - 1) % nrow
+        for d in range(1, ncol):
+            pl.semaphore_signal(barrier, inc=1, device_id=(r, (k + d) % ncol), device_id_type=MESH)
+        for d in range(ncol):
+            pl.semaphore_signal(barrier, inc=1, device_id=(up, (k + d) % ncol), device_id_type=MESH)
+            pl.semaphore_signal(barrier, inc=1, device_id=(down, (k + d) % ncol), device_id_type=MESH)
+    else:
+        sends, relays, peers = plan
+        for row, col in sorted(peers):
+
+            @pl.when(me == row * ncol + col)
+            def _(others=sorted(peers[row, col])):
+                for other in others:
+                    pl.semaphore_signal(barrier, inc=1, device_id=other, device_id_type=MESH)
 
     lane = lax.broadcasted_iota(jnp.int32, (1, LANES), 1)
 
     def mask(l, t):
         for b in range(blocks):
-            p0 = pattern_ref[l * blocks + b, 2 * t].astype(jnp.float32)
-            p1 = pattern_ref[l * blocks + b, 2 * t + 1].astype(jnp.float32)
+            p0 = pattern_ref[2 * t, l * blocks + b].astype(jnp.float32)
+            p1 = pattern_ref[2 * t + 1, l * blocks + b].astype(jnp.float32)
             rows = pl.ds(b * BLOCK, BLOCK)
             stage[l, t, rows, :] = stage[l, t, rows, :] * jnp.where(lane < BLOCK, p0, p1)
 
@@ -81,7 +169,8 @@
         return carry
 
     lax.fori_loop(0, ncol, mask_all, 0)
-    pl.semaphore_wait(barrier, 3 * ncol - 1)
+    if plan is None:
+        pl.semaphore_wait(barrier, 3 * ncol - 1)
 
     def send_all(l, carry):
         for t in range(per):
@@ -91,8 +180,50 @@
                 pl.when(remote)(move.start)
         return carry
 
-    lax.fori_loop(0, ncol, send_all, 0)
+    def routed(row, col, n):
+        l, t, h, j, to_row, to_col, slot = sends[row, col][n]
+        if (to_row, to_col) == (row, col):
+            return pltpu.make_async_copy(stage.at[l, t], recv.at[h, j], recv_sem.at[h, j])
+        return pltpu.make_async_remote_copy(
+            stage.at[l, t], recv.at[h, j] if slot is None else hold.at[slot], send_sem.at[l, t, h // 2],
+            recv_sem.at[h, j] if slot is None else hold_sem.at[slot],
+            device_id=(to_row, to_col), device_id_type=MESH,
+        )
+
+    def relayed(row, col, slot):
+        h, j, to_row, to_col = relays[row, col][slot]
+        return pltpu.make_async_remote_copy(
+            hold.at[slot], recv.at[h, j], via_sem.at[slot], recv_sem.at[h, j],
+            device_id=(to_row, to_col), device_id_type=MESH,
+        )
+
+    def taken(slot):
+        return pltpu.make_async_remote_copy(
+            hold.at[slot], hold.at[slot], via_sem.at[slot], hold_sem.at[slot],
+            device_id=(r, k + 1 - 2 * core), device_id_type=MESH,
+        )
+
+    if plan is None:
+        lax.fori_loop(0, ncol, send_all, 0)
+    else:
+        for row, col in sorted(peers):
+
+            @pl.when(me == row * ncol + col)
+            def _(row=row, col=col):
+                pl.semaphore_wait(barrier, len(peers[row, col]))
+                for n in range(len(sends.get((row, col), ()))):
+                    routed(row, col, n).start()
+
     out_ref[...] = jnp.zeros_like(out_ref)
+    if plan is not None:
+        for row, col in sorted(relays):
+
+            @pl.when(me == row * ncol + col)
+            def _(row=row, col=col):
+                for slot in range(len(relays[row, col])):
+                    taken(slot).wait_recv()
+                    relayed(row, col, slot).start()
+
 
     def pass_on(h, j):
         return pltpu.make_async_remote_copy(
@@ -148,7 +279,19 @@
                 pl.when(remote)(move.wait_send)
         return carry
 
-    lax.fori_loop(0, ncol, sent_all, 0)
+    if plan is None:
+        lax.fori_loop(0, ncol, sent_all, 0)
+    else:
+        for row, col in sorted(peers):
+
+            @pl.when(me == row * ncol + col)
+            def _(row=row, col=col):
+                for n, move in enumerate(sends.get((row, col), ())):
+                    if move[4:6] != (row, col):
+                        routed(row, col, n).wait_send()
+                for slot in range(len(relays.get((row, col), ()))):
+                    relayed(row, col, slot).wait_send()
+
 
     def passed_all(j, carry):
         pl.when(j >= jnp.where(shared < 2, 0, late))(pass_on(shared, j).wait_send)
@@ -163,20 +306,27 @@
     nbr, nbo = pattern.shape[0] * nrow, pattern.shape[1] * ncol
     per = cols // LANES
     span = REACH + 1
+    plan, held = None, 1
+    if (nrow, ncol) == (8, 4):
+        plan = planned(nrow, ncol, per, width, nbr, nbo, span, 1 if width // BLOCK * nbo == nbr else 0)
+        held = max([1] + [len(moves) for moves in plan[1].values()])
     return pl.pallas_call(
-        functools.partial(kernel, nrow, ncol, nbr, nbo),
+        functools.partial(kernel, nrow, ncol, nbr, nbo, plan),
         out_shape=jax.ShapeDtypeStruct((1, STEPS, width, width), jnp.float32),
-        in_specs=[pl.BlockSpec(memory_space=pl.ANY), pl.BlockSpec(memory_space=pltpu.SMEM)],
+        in_specs=[pl.BlockSpec(memory_space=pltpu.HBM), pl.BlockSpec(memory_space=pltpu.SMEM)],
         out_specs=pl.BlockSpec(memory_space=pltpu.VMEM),
         scratch_shapes=[
             pltpu.VMEM((ncol, per, width, LANES), jnp.float32),
             pltpu.VMEM((4, span, width, LANES), jnp.float32),
+            pltpu.VMEM((held, width, LANES), jnp.float32),
             pltpu.VMEM((width, 3 * LANES), jnp.bfloat16),
             pltpu.VMEM((width, 3 * LANES), jnp.bfloat16),
             pltpu.SemaphoreType.DMA((ncol, per)),
             pltpu.SemaphoreType.DMA((ncol, per, 2)),
             pltpu.SemaphoreType.DMA((4, span)),
             pltpu.SemaphoreType.DMA((span,)),
+            pltpu.SemaphoreType.DMA((held,)),
+            pltpu.SemaphoreType.DMA((held,)),
         ],
         compiler_params=pltpu.CompilerParams(
             collective_id=0, has_side_effects=True, vmem_limit_bytes=40 << 20
@@ -185,7 +335,7 @@
             flops=2 * 3 * STEPS * width * width * span * LANES,
             bytes_accessed=4 * (rows * cols + STEPS * width * width), transcendentals=0,
         ),
-    )(coeffs, pattern)
+    )(coeffs, pattern.T)
 
 
 def solution(mesh):

time: 78.4 us -> 67.4 us (0.86)
  the two profiles are of different devices: /device:TPU:6 before, /device:TPU:2 now
where the time goes in v2:
time: 67.4 us; the launch traced here: 67.2 us
  Pallas kernels  62.6 us (93%)
  local copies, waits for them, and re-layouts  4.54 us (7%)
    pallas_call x1, Pallas kernels, shards(): pl.pallas_call(functools.partial(kernel, nrow, ncol, nbr, nbo, plan), out...  62.6 us
    unnamed x5, local copies, waits for them, and re-layouts  4.54 us

profile of v2, /device:TPU:2, one launch (start us, length us, event | category | flops | bytes accessed | tf_op | source)
XLA Modules:
  0.0 67.2 jit_solution(2371888745603349589)
XLA Ops:
  0.0 0.0 copy-start
  0.0 2.2 %copy-done = f32[2048,512]{1,0:T(8,128)S(1)} copy-done((f32[2048,512]{1,0:T(8,128)S(1)}, f32[2048,512]{1,0:T(8,128)}, u32[]{:S(2)}) %copy-start) | copy-done | bytes 4194328
  2.2 0.0 copy-start.1
  2.2 0.7 %copy-done.1 = s32[32,8]{0,1:T(8,128)S(1)} copy-done((s32[32,8]{0,1:T(8,128)S(1)}, s32[32,8]{0,1:T(8,128)}, u32[]{:S(2)}) %copy-start.1) | copy-done | bytes 1048
  2.9 62.6 %shard_map.28 = f32[1,3,512,512]{3,2,1,0:T(8,128)S(1)} custom-call(f32[2048,512]{1,0:T(8,128)S(1)} %copy-done, s32[8,32]{1,0:T(8,128)S(1)} %bitcast.1), custom_call_target="tpu_custom_call" | custom-call | flops 3019898880 | bytes 7340032 | tf_op jit(solution)/shard_map/pallas_call | solution.py:313
  65.5 1.7 %copy.4 = f32[1,3,512,512]{3,2,1,0:T(8,128)} copy(f32[1,3,512,512]{3,2,1,0:T(8,128)S(1)} %shard_map.28) | data formatting | bytes 6291456
Async XLA Ops:
  0.0 2.2 %copy-start = (f32[2048,512]{1,0:T(8,128)S(1)}, f32[2048,512]{1,0:T(8,128)}, u32[]{:S(2)}) copy-start(f32[2048,512]{1,0:T(8,128)} %coeffs_ref.1) | copy-start | bytes 12582916
  2.2 0.7 %copy-start.1 = (s32[32,8]{0,1:T(8,128)S(1)}, s32[32,8]{0,1:T(8,128)}, u32[]{:S(2)}) copy-start(s32[32,8]{0,1:T(8,128)} %param.3) | copy-start | bytes 3076

commit v3 on v2

--- a/solution.py
+++ b/solution.py
@@ -258,15 +258,12 @@
                 right[:, LANES:2 * LANES] = high
                 right[:, 2 * LANES:3 * LANES] = low
 
-                def part(i, carry):
-                    rows = pl.ds(pl.multiple_of(i * LANES, LANES), LANES)
-                    out_ref[0, step, rows, :] += lax.dot_general(
-                        left[rows, :], right[...], (((1,), (1,)), ((), ())),
+                for i in range(2):
+                    cols = pl.ds(i * (width // 2), width // 2)
+                    out_ref[0, step, :, cols] += lax.dot_general(
+                        left[...], right[cols, :], (((1,), (1,)), ((), ())),
                         preferred_element_type=jnp.float32,
                     )
-                    return carry
-
-                lax.fori_loop(0, width // LANES, part, 0)
 
         return carry
 

time: 67.4 us -> 59.9 us (0.89)
  Pallas kernels: 62.6 us -> 55.2 us
    pallas_call x1, Pallas kernels: 62.6 us -> 55.2 us  [shards(): pl.pallas_call(functools.partial(kernel, nrow, ncol, nbr, nbo, plan), out...]
where the time goes in v3:
time: 59.9 us; the launch traced here: 59.8 us
  Pallas kernels  55.2 us (92%)
  local copies, waits for them, and re-layouts  4.54 us (8%)
    pallas_call x1, Pallas kernels, shards(): pl.pallas_call(functools.partial(kernel, nrow, ncol, nbr, nbo, plan), out...  55.2 us
    unnamed x5, local copies, waits for them, and re-layouts  4.54 us

profile of v3, /device:TPU:2, one launch (start us, length us, event | category | flops | bytes accessed | tf_op | source)
XLA Modules:
  0.0 59.8 jit_solution(15317719811616392693)
XLA Ops:
  0.0 0.0 copy-start
  0.0 2.2 %copy-done = f32[2048,512]{1,0:T(8,128)S(1)} copy-done((f32[2048,512]{1,0:T(8,128)S(1)}, f32[2048,512]{1,0:T(8,128)}, u32[]{:S(2)}) %copy-start) | copy-done | bytes 4194328
  2.2 0.0 copy-start.1
  2.2 0.7 %copy-done.1 = s32[32,8]{0,1:T(8,128)S(1)} copy-done((s32[32,8]{0,1:T(8,128)S(1)}, s32[32,8]{0,1:T(8,128)}, u32[]{:S(2)}) %copy-start.1) | copy-done | bytes 1048
  2.9 55.2 %shard_map.28 = f32[1,3,512,512]{3,2,1,0:T(8,128)S(1)} custom-call(f32[2048,512]{1,0:T(8,128)S(1)} %copy-done, s32[8,32]{1,0:T(8,128)S(1)} %bitcast.1), custom_call_target="tpu_custom_call" | custom-call | flops 3019898880 | bytes 7340032 | tf_op jit(solution)/shard_map/pallas_call | solution.py:310
  58.1 1.7 %copy.4 = f32[1,3,512,512]{3,2,1,0:T(8,128)} copy(f32[1,3,512,512]{3,2,1,0:T(8,128)S(1)} %shard_map.28) | data formatting | bytes 6291456
Async XLA Ops:
  0.0 2.2 %copy-start = (f32[2048,512]{1,0:T(8,128)S(1)}, f32[2048,512]{1,0:T(8,128)}, u32[]{:S(2)}) copy-start(f32[2048,512]{1,0:T(8,128)} %coeffs_ref.1) | copy-start | bytes 12582916
  2.2 0.7 %copy-start.1 = (s32[32,8]{0,1:T(8,128)S(1)}, s32[32,8]{0,1:T(8,128)}, u32[]{:S(2)}) copy-start(s32[32,8]{0,1:T(8,128)} %param.3) | copy-start | bytes 3076

commit v4 on v3

--- a/solution.py
+++ b/solution.py
@@ -55,7 +55,7 @@
         for i, ways in enumerate(choices):
             load.subtract(ways[chosen[i]][1])
             costs = [
-                (sum((load[e] + 1) ** 6 - load[e] ** 6 for e in way) + (0 if q is None else 72900), n != chosen[i], n)
+                (sum((load[e] + 1) ** 6 - load[e] ** 6 for e in way) + (0 if q is None else 729), n != chosen[i], n)
                 for n, (q, way) in enumerate(ways)
             ]
             chosen[i] = min(costs)[2]
@@ -63,7 +63,7 @@
     sends = collections.defaultdict(list)
     relays = collections.defaultdict(list)
     used = collections.Counter()
-    order = sorted(range(len(tiles)), key=lambda i: (chosen[i] == 0, tiles[i][5], i))
+    order = sorted(range(len(tiles)), key=lambda i: (chosen[i] == 0, tiles[i][5], tiles[i][4], i))
     for i in order:
         row, k, l, t, h, j, to_row, to_col = tiles[i]
         q = choices[i][chosen[i]][0]

time: 59.9 us -> 57.7 us (0.963)
  Pallas kernels: 55.2 us -> 53 us
    pallas_call x1, Pallas kernels: 55.2 us -> 53 us  [shards(): pl.pallas_call(functools.partial(kernel, nrow, ncol, nbr, nbo, plan), out...]
where the time goes in v4:
time: 57.7 us; the launch traced here: 57.5 us
  Pallas kernels  53 us (92%)
  local copies, waits for them, and re-layouts  4.54 us (8%)
    pallas_call x1, Pallas kernels, shards(): pl.pallas_call(functools.partial(kernel, nrow, ncol, nbr, nbo, plan), out...  53 us
    unnamed x5, local copies, waits for them, and re-layouts  4.54 us

profile of v4, /device:TPU:2, one launch (start us, length us, event | category | flops | bytes accessed | tf_op | source)
XLA Modules:
  0.0 57.5 jit_solution(13622012337927914484)
XLA Ops:
  0.0 0.0 copy-start
  0.0 2.2 %copy-done = f32[2048,512]{1,0:T(8,128)S(1)} copy-done((f32[2048,512]{1,0:T(8,128)S(1)}, f32[2048,512]{1,0:T(8,128)}, u32[]{:S(2)}) %copy-start) | copy-done | bytes 4194328
  2.2 0.0 copy-start.1
  2.2 0.7 %copy-done.1 = s32[32,8]{0,1:T(8,128)S(1)} copy-done((s32[32,8]{0,1:T(8,128)S(1)}, s32[32,8]{0,1:T(8,128)}, u32[]{:S(2)}) %copy-start.1) | copy-done | bytes 1048
  2.9 53.0 %shard_map.28 = f32[1,3,512,512]{3,2,1,0:T(8,128)S(1)} custom-call(f32[2048,512]{1,0:T(8,128)S(1)} %copy-done, s32[8,32]{1,0:T(8,128)S(1)} %bitcast.1), custom_call_target="tpu_custom_call" | custom-call | flops 3019898880 | bytes 7340032 | tf_op jit(solution)/shard_map/pallas_call | solution.py:310
  55.9 1.7 %copy.4 = f32[1,3,512,512]{3,2,1,0:T(8,128)} copy(f32[1,3,512,512]{3,2,1,0:T(8,128)S(1)} %shard_map.28) | data formatting | bytes 6291456
Async XLA Ops:
  0.0 2.2 %copy-start = (f32[2048,512]{1,0:T(8,128)S(1)}, f32[2048,512]{1,0:T(8,128)}, u32[]{:S(2)}) copy-start(f32[2048,512]{1,0:T(8,128)} %coeffs_ref.1) | copy-start | bytes 12582916
  2.2 0.7 %copy-start.1 = (s32[32,8]{0,1:T(8,128)S(1)}, s32[32,8]{0,1:T(8,128)}, u32[]{:S(2)}) copy-start(s32[32,8]{0,1:T(8,128)} %param.3) | copy-start | bytes 3076
